TPU v7x, 32 devices: a whole 2x2x4 slice. The times are simulated.
32 devices in a mesh: node: 8 (over y, x, core), group: 4 (over z).
Axes of the slice: x: 2, y: 2, z: 4, core: 2. Of those that a mesh axis runs over, the one named last changes fastest.
Arguments:
- tokens: bfloat16 [1024, 3584], P('node', 'group'), may hold values from -10 to 10
- node_routes: int32 [1024, 4], P('node'), may hold values from 0 to 7, all different within a row; in each aligned block of 128 rows (0 to 127, 128 to 255, ...) at most 128 rows name the same one
- combine: int32 [1024, 8], P('node'), may hold values from 64 to 256
- w_gate: bfloat16 [3584, 16384], P(None, ('node', 'group')), may hold values from -0.09375 to 0.09375
- w_up: bfloat16 [3584, 16384], P(None, ('node', 'group')), may hold values from -0.09375 to 0.09375
- w_down: bfloat16 [3584, 16384], P('group', 'node'), may hold values from -0.1875 to 0.1875
Outputs:
- moe_out: bfloat16 [1024, 3584], P('node', 'group')
Inputs may be any that keep to these rules, and one draw needn't show every extreme that they name: `node_routes`: each token names 4 different nodes. Among the 128 tokens of one node (rows n * 128 to (n + 1) * 128 - 1) no node is named by more than 128 tokens, a bound that some block reaches of them.
All inputs are finite; a program needn't handle non-finite values.
Results may differ from a plain program's by a relative error of at most 0.0057.
Values may be sent and summed in bfloat16 or wider, within the bound.
A program may use at most 64 MiB of HBM per device.

v0:
```python
import jax
import jax.numpy as jnp
from jax import lax
from jax.sharding import PartitionSpec as P

F = 1024
EXP_NODE = 2


def shards(tokens, node_routes, combine, w_gate, w_up, w_down):
    node_count = lax.axis_size("node")
    tok_count = tokens.shape[0]
    col_width = tokens.shape[1]
    hid_dev = w_gate.shape[1]
    slots = 2 * tok_count * node_routes.shape[1] // node_count
    row_total = node_count * slots
    targets = jnp.arange(node_count, dtype=jnp.int32)
    node_hits = (node_routes[:, :, None] == targets[None, None, :]).astype(jnp.float32)
    member = jnp.sum(node_hits, axis=1)
    slot_rank = jnp.cumsum(member, axis=0) - member
    slot_numbers = jnp.arange(slots, dtype=jnp.float32)
    placed = member[:, :, None] * (slot_rank[:, :, None] == slot_numbers).astype(jnp.float32)
    pair_weights = combine.reshape(tok_count, -1, EXP_NODE).astype(jnp.float32) / 1024.0
    node_pair = jnp.einsum("tjm,tjk->tmk", node_hits, pair_weights)
    slot_weights = jnp.einsum("tmc,tmk->mck", placed, node_pair).astype(jnp.bfloat16)
    placed_low = placed.astype(jnp.bfloat16)
    send_rows = jnp.einsum(
        "tmc,td->mcd", placed_low, tokens, preferred_element_type=jnp.float32
    ).astype(jnp.bfloat16)
    send_rows = send_rows.reshape(node_count, slots * col_width)
    got_rows, got_weights = (
        lax.all_to_all(send_rows, "node", split_axis=0, concat_axis=0, tiled=True),
        lax.all_to_all(slot_weights, "node", split_axis=0, concat_axis=0, tiled=True),
    )
    node_rows = got_rows.reshape(row_total, col_width)
    weight_rows = got_weights.reshape(row_total, EXP_NODE).astype(jnp.float32)
    local_expert = lax.axis_index("group") * hid_dev // F
    expert_pick = (jnp.arange(EXP_NODE, dtype=jnp.int32) == local_expert).astype(jnp.float32)
    row_scale = jnp.sum(weight_rows * expert_pick[None, :], axis=1)
    whole_rows = lax.all_gather(node_rows, "group", axis=1, tiled=True)
    gate_acts = jnp.dot(whole_rows, w_gate, preferred_element_type=jnp.float32)
    up_acts = jnp.dot(whole_rows, w_up, preferred_element_type=jnp.float32)
    hidden = (row_scale[:, None] * jax.nn.silu(gate_acts) * up_acts).astype(jnp.bfloat16)
    contract = (((1,), (1,)), ((), ()))
    all_hidden = lax.all_gather(hidden, "group", axis=1, tiled=True)
    out_back = lax.dot_general(w_down, all_hidden, contract, preferred_element_type=jnp.float32)
    out_back = out_back.astype(jnp.bfloat16)
    returned = lax.all_to_all(out_back, "node", split_axis=1, concat_axis=1, tiled=True)
    mixed_out = lax.dot_general(
        placed_low.reshape(tok_count, row_total),
        returned,
        contract,
        preferred_element_type=jnp.float32,
    )
    return mixed_out.astype(jnp.bfloat16)


def solution(mesh):
    in_specs = (
        P("node", "group"),
        P("node", None),
        P("node", None),
        P(None, ("node", "group")),
        P(None, ("node", "group")),
        P("group", "node"),
    )
    out_specs = P("node", "group")
    return jax.shard_map(shards, mesh=mesh, in_specs=in_specs, out_specs=out_specs, check_vma=False)
```

profile of v0, /device:TPU:1, one launch (start us, length us, event | category | flops | bytes accessed | tf_op | source)
XLA Modules:
  0.0 349.7 jit_solution(96568725898157075)
XLA Ops:
  6.5 0.0 copy-start
  6.5 0.0 all-gather.3.cloned.1.call-start
  6.5 0.8 copy.18
  7.4 0.3 convert_reduce_fusion
  7.6 0.1 copy.20
  7.7 0.2 reduce_window_sum.11
  7.9 0.0 copy-done
  7.9 1.1 convolution_convert_fusion.1
  9.0 3.6 %all_to_all.20 = bf16[8,1,114688]{2,1,0:T(2,128)(2,1)} reshape(bf16[8,128,896]{2,1,0:T(8,128)(2,1)S(1)} %convolution_convert_fusion.1) | data formatting | bytes 3670016 | tf_op jit(solution)/shard_map/all_to_all | solution.py:32
  12.7 0.5 broadcast.33
  13.2 13.7 %reduce.2 = bf16[8,114688]{1,0:T(8,128)(2,1)} reduce(bf16[8,1,114688]{2,1,0:T(2,128)(2,1)} %all_to_all.20, bf16[]{:T(256)} %broadcast.33), dimensions={1}, to_apply=%all_to_all.20.reduce_sub_computation | reduce | bytes 3670018 | tf_op jit(solution)/shard_map/all_to_all | solution.py:32
  26.8 3.1 reshape.44
  29.9 27.6 %all_to_all.24 = bf16[8,2,57344]{2,1,0:T(2,128)(2,1)} all-to-all(bf16[8,2,57344]{2,1,0:T(2,128)(2,1)S(1)} %reshape.44), channel_id=1, replica_groups=mesh['node'=8,'group'=4] {'node'}, dimensions={0} | all-to-all | bytes 3670016 | tf_op jit(solution)/shard_map/all_to_all | solution.py:32
  57.5 6.6 %reshape.45 = bf16[8,1,114688]{2,1,0:T(2,128)(2,1)} reshape(bf16[8,2,57344]{2,1,0:T(2,128)(2,1)} %all_to_all.24) | data formatting | bytes 3670016
  64.1 11.8 %reduce.1 = bf16[8,114688]{1,0:T(8,128)(2,1)S(1)} reduce(bf16[8,1,114688]{2,1,0:T(2,128)(2,1)} %reshape.45, bf16[]{:T(256)} %constant.34), dimensions={1}, to_apply=%all_to_all.17.reduce_sub_computation | reduce | bytes 3670018 | tf_op jit(solution)/shard_map/all_to_all | solution.py:32
  75.9 0.0 copy-start.1
  75.9 2.2 reshape.40
  78.1 0.0 all-gather.3.cloned.1.call-update
  78.1 0.0 copy-done.1
  78.1 0.1 copy.21
  78.3 0.3 fusion.11
  78.6 0.1 copy.22
  78.7 1.1 convolution_convert_fusion.2
  79.8 4.5 %all-to-all-start = ((bf16[8,128,2]{1,2,0:T(2,128)(2,1)}), bf16[8,128,2]{1,2,0:T(2,128)(2,1)S(1)}, u32[]{:S(2)}, u32[]{:S(2)}) async-start(bf16[8,128,2]{1,2,0:T(2,128)(2,1)} %convolution_convert_fusion.2), calls=%async_computation | async-start | bytes 8192 | tf_op jit(solution)/shard_map/all_to_all | solution.py:33
  84.3 0.0 all-gather.5.cloned.1.call-start
  84.3 3.9 %all-to-all-done = bf16[8,128,2]{1,2,0:T(2,128)(2,1)S(1)} async-done(((bf16[8,128,2]{1,2,0:T(2,128)(2,1)}), bf16[8,128,2]{1,2,0:T(2,128)(2,1)S(1)}, u32[]{:S(2)}, u32[]{:S(2)}) %all-to-all-start) | async-done | bytes 4128 | tf_op jit(solution)/shard_map/all_to_all | solution.py:33
  88.2 0.1 multiply_reduce_fusion
  88.3 122.7 %all-gather.3.cloned.1.call-done = bf16[1024,3584]{1,0:T(8,128)(2,1)} async-done(((bf16[1024,896]{1,0:T(8,128)(2,1)}), bf16[1024,3584]{1,0:T(8,128)(2,1)}) %all-gather.3.cloned.1.call-update) | async-done | bytes 7340048 | tf_op jit(solution)/shard_map/all_gather | solution.py:40
  211.0 0.0 copy-start.2
  211.0 0.0 copy-start.3
  211.0 7.4 %fusion.17 = f32[1024,512]{1,0:T(8,128)S(1)} fusion(bf16[1024,3584]{1,0:T(8,128)(2,1)} %all-gather.3.cloned.1.call-done, bf16[3584,512]{1,0:T(8,128)(2,1)} %param.9), kind=kOutput, calls=%fused_computation.29 | convolution fusion | flops 3758096384 | bytes 13107200 | tf_op jit(solution)/shard_map/dot_general | solution.py:41
  218.4 0.0 copy-done.2
  218.4 0.0 copy-done.3
  218.4 5.2 %multiply_convert_fusion = bf16[1024,512]{1,0:T(8,128)(2,1)} fusion(f32[1024,512]{1,0:T(8,128)S(1)} %fusion.17, bf16[1024,3584]{1,0:T(8,128)(2,1)S(1)} %copy-done.2, bf16[3584,512]{1,0:T(8,128)(2,1)S(1)} %copy-done.3, f32[1024]{0:T(1024)S(1)} %bitcast.23), kind=kOutput, calls=%fused_computation | convolution fusion | flops 3761766400 | bytes 14159872 | tf_op jit(solution)/shard_map/dot_general | solution.py:42
  223.6 0.0 all-gather.5.cloned.1.call-update
  223.6 78.9 %all-gather.5.cloned.1.call-done = bf16[1024,2048]{1,0:T(8,128)(2,1)} async-done(((bf16[1024,512]{1,0:T(8,128)(2,1)}), bf16[1024,2048]{1,0:T(8,128)(2,1)}) %all-gather.5.cloned.1.call-update) | async-done | bytes 4194320 | tf_op jit(solution)/shard_map/all_gather | solution.py:45
  302.5 9.1 %convolution_convert_fusion = bf16[1024,896]{1,0:T(8,128)(2,1)} fusion(bf16[1024,2048]{1,0:T(8,128)(2,1)} %all-gather.5.cloned.1.call-done, bf16[896,2048]{1,0:T(8,128)(2,1)} %param.11), kind=kOutput, calls=%fused_computation.1 | convolution fusion | flops 3759013888 | bytes 9699328 | tf_op jit(solution)/shard_map/dot_general | solution.py:46
  311.6 3.2 copy.25
  314.8 26.6 %all_to_all.25 = bf16[896,8,128]{2,0,1:T(8,128)(2,1)S(1)} all-to-all(bf16[896,8,128]{2,0,1:T(8,128)(2,1)S(1)} %copy.25), channel_id=1, replica_groups=mesh['node'=8,'group'=4] {'node'}, dimensions={1} | all-to-all | bytes 3670016 | tf_op jit(solution)/shard_map/all_to_all | solution.py:48
  341.4 1.4 fusion
  (4 shorter events, 0.1 us)
Async XLA Ops:
  6.5 1.4 copy-start
  6.5 204.4 %all-gather.3.cloned.1.call-start = ((), (), s32[]{:S(2)}) async-start(), calls=%async_computation.3 | async-start | bytes 9175040 | tf_op jit(solution)/shard_map/all_gather | solution.py:40
  75.9 2.2 copy-start.1
  79.8 8.5 %all-to-all-start = ((bf16[8,128,2]{1,2,0:T(2,128)(2,1)}), bf16[8,128,2]{1,2,0:T(2,128)(2,1)S(1)}, u32[]{:S(2)}, u32[]{:S(2)}) async-start(bf16[8,128,2]{1,2,0:T(2,128)(2,1)} %convolution_convert_fusion.2), calls=%async_computation | async-start | bytes 8192 | tf_op jit(solution)/shard_map/all_to_all | solution.py:33
  84.3 218.2 %all-gather.5.cloned.1.call-start = ((), (), s32[]{:S(2)}) async-start(), calls=%async_computation.4 | async-start | bytes 5242880 | tf_op jit(solution)/shard_map/all_gather | solution.py:45
  211.0 7.4 %copy-start.2 = (bf16[1024,3584]{1,0:T(8,128)(2,1)S(1)}, bf16[1024,3584]{1,0:T(8,128)(2,1)}, u32[]{:S(2)}) copy-start(bf16[1024,3584]{1,0:T(8,128)(2,1)} %all-gather.3.cloned.1.call-done) | copy-start | bytes 22020100
  211.0 7.4 %copy-start.3 = (bf16[3584,512]{1,0:T(8,128)(2,1)S(1)}, bf16[3584,512]{1,0:T(8,128)(2,1)}, u32[]{:S(2)}) copy-start(bf16[3584,512]{1,0:T(8,128)(2,1)} %param.10) | copy-start | bytes 11010052
Sparse Core Ops, SparseCore 0:
  78.2 132.7 all-gather.2
  223.8 78.7 all-gather.4
where the time goes:
time: 351 us; the launch traced here: 350 us
  waiting for transfers between devices  206 us (59%)
  blocking collectives  54.2 us (15%)
  other arithmetic  26 us (7%)
  matrix products  25.6 us (7%)
  local copies, waits for them, and re-layouts  20.3 us (6%)
  between operations  13.5 us (4%)
  starting transfers between devices  4.55 us (1%)
    all_gather x1, waiting for transfers between devices, shards(): whole_rows = lax.all_gather(node_rows, 'group', axis=1, tiled=True)  123 us
    all_gather x1, waiting for transfers between devices, shards(): all_hidden = lax.all_gather(hidden, 'group', axis=1, tiled=True)  78.9 us
    all_to_all x1, blocking collectives, shards(): lax.all_to_all(send_rows, 'node', split_axis=0, concat_axis=0, tiled=True)  27.6 us
    all_to_all x1, blocking collectives, shards(): lax.all_to_all(out_back, 'node', split_axis=1, concat_axis=1, tiled=True)  26.6 us
    all_to_all x2, other arithmetic, shards(): lax.all_to_all(send_rows, 'node', split_axis=0, concat_axis=0, tiled=True)  25.4 us
    unnamed x11, local copies, waits for them, and re-layouts  10.5 us
    dot_general x1, matrix products, shards(): lax.dot_general(w_down, all_hidden, contract, preferred_element_type=jnp....  9.11 us
    dot_general x1, matrix products, shards(): gate_acts = jnp.dot(whole_rows, w_gate, preferred_element_type=jnp.float32)  7.42 us
  transfers between devices with their start and end apart: 3, of which 3 were waited for; matrix products, arithmetic and copies ran while one was open for 0% of the time, Pallas kernels for 0%

commit v1 on v0

--- a/solution.py
+++ b/solution.py
@@ -7,7 +7,7 @@
 EXP_NODE = 2
 
 
-def shards(tokens, node_routes, combine, w_gate, w_up, w_down):
+def routed_shards(tokens, node_routes, combine, w_gate, w_up, w_down):
     node_count = lax.axis_size("node")
     tok_count = tokens.shape[0]
     col_width = tokens.shape[1]
@@ -55,6 +55,38 @@
     return mixed_out.astype(jnp.bfloat16)
 
 
+def pair_scales(node_routes, combine):
+    node_count = lax.axis_size("node")
+    targets = jnp.arange(node_count, dtype=jnp.int32)
+    hits = (node_routes[:, :, None] == targets[None, None, :]).astype(jnp.float32)
+    pairs = combine.reshape(combine.shape[0], -1, EXP_NODE).astype(jnp.float32) / 1024.0
+    return jnp.einsum("tjm,tjk->tmk", hits, pairs).reshape(combine.shape[0], -1)
+
+
+def dense_shards(tokens, node_routes, combine, w_gate, w_up, w_down):
+    hid_dev = w_gate.shape[1]
+    scales = pair_scales(node_routes, combine).astype(jnp.bfloat16)
+    all_scales = lax.all_gather(scales, "node", axis=0, tiled=True)
+    column = lax.all_gather(tokens, "group", axis=1, tiled=True)
+    rows = lax.all_gather(column, "node", axis=0, tiled=True)
+    expert = EXP_NODE * lax.axis_index("node") + lax.axis_index("group") * hid_dev // F
+    row_scale = lax.dynamic_slice_in_dim(all_scales, expert, 1, 1).astype(jnp.float32)
+    gate_acts = jnp.dot(rows, w_gate, preferred_element_type=jnp.float32)
+    up_acts = jnp.dot(rows, w_up, preferred_element_type=jnp.float32)
+    hidden = (row_scale * jax.nn.silu(gate_acts) * up_acts).astype(jnp.bfloat16)
+    all_hidden = lax.all_gather(hidden, "group", axis=1, tiled=True)
+    contract = (((1,), (1,)), ((), ()))
+    part = lax.dot_general(all_hidden, w_down, contract, preferred_element_type=jnp.float32)
+    return lax.psum_scatter(part.astype(jnp.bfloat16), "node", scatter_dimension=0, tiled=True)
+
+
+def shards(tokens, node_routes, *rest):
+    slots = 2 * tokens.shape[0] * node_routes.shape[1] // lax.axis_size("node")
+    if slots == tokens.shape[0]:
+        return dense_shards(tokens, node_routes, *rest)
+    return routed_shards(tokens, node_routes, *rest)
+
+
 def solution(mesh):
     in_specs = (
         P("node", "group"),

time: 351 us -> 227 us (0.65)
  waiting for transfers between devices: 206 us -> 157 us
  other arithmetic: 26 us -> 0.7 us
  blocking collectives: 54.2 us -> 32.3 us
  local copies, waits for them, and re-layouts: 20.3 us -> 1.01 us
  starting transfers between devices: 4.55 us -> 0.09 us
  matrix products: 25.6 us -> 22 us
    all_gather x2, waiting for transfers between devices: 202 us -> 119 us  [the longest x1 80.5 us: dense_shards(): all_hidden = lax.all_gather(hidden, 'group', axis=1, tiled=True)]
    all_to_all x2 -> x0, blocking collectives: 54.2 us -> none  [the longest x1 27.6 us: shards(): lax.all_to_all(send_rows, 'node', split_axis=0, concat_axis=0, tiled=True)]
    reduce_scatter x0 -> x1, waiting for transfers between devices: none -> 38.3 us  [dense_shards(): lax.psum_scatter(part.astype(jnp.bfloat16), 'node', scatter_dimension=0,...]
    all_gather x0 -> x2, blocking collectives: none -> 32.3 us  [the longest x1 20.9 us: dense_shards(): column = lax.all_gather(tokens, 'group', axis=1, tiled=True)]
    all_to_all x2 -> x0, other arithmetic: 25.4 us -> none  [shards(): lax.all_to_all(send_rows, 'node', split_axis=0, concat_axis=0, tiled=True)]
    unnamed x11 -> x5, local copies, waits for them, and re-layouts: 10.5 us -> 0.8 us
    all_to_all x3 -> x0, local copies, waits for them, and re-layouts: 7.31 us -> none  [the longest x2 4.15 us: shards(): lax.all_to_all(send_rows, 'node', split_axis=0, concat_axis=0, tiled=True)]
    all_to_all x1 -> x0, starting transfers between devices: 4.54 us -> none  [shards(): lax.all_to_all(slot_weights, 'node', split_axis=0, concat_axis=0, tiled=T...]
  transfers between devices with their start and end apart: 3 -> 3, of which waited for: 3 -> 3; matrix products, arithmetic and copies ran while one was open for 0% -> 1% of each run, Pallas kernels for 0% -> 0%
where the time goes in v1:
time: 227 us
  waiting for transfers between devices  157 us (69%)
  blocking collectives  32.3 us (14%)
  matrix products  22 us (10%)
  between operations  13.2 us (6%)
    all_gather x1, waiting for transfers between devices, dense_shards(): all_hidden = lax.all_gather(hidden, 'group', axis=1, tiled=True)  80.5 us
    all_gather x1, waiting for transfers between devices, dense_shards(): rows = lax.all_gather(column, 'node', axis=0, tiled=True)  38.4 us
    reduce_scatter x1, waiting for transfers between devices, dense_shards(): lax.psum_scatter(part.astype(jnp.bfloat16), 'node', scatter_dimension=0,...  38.3 us
    all_gather x1, blocking collectives, dense_shards(): column = lax.all_gather(tokens, 'group', axis=1, tiled=True)  20.9 us
    all_gather x1, blocking collectives, dense_shards(): all_scales = lax.all_gather(scales, 'node', axis=0, tiled=True)  11.5 us
    dot_general x1, matrix products, dense_shards(): lax.dot_general(all_hidden, w_down, contract, preferred_element_type=jnp....  9.1 us
    dot_general x1, matrix products, dense_shards(): gate_acts = jnp.dot(rows, w_gate, preferred_element_type=jnp.float32)  7.42 us
    dot_general x1, matrix products, dense_shards(): up_acts = jnp.dot(rows, w_up, preferred_element_type=jnp.float32)  5.16 us
  transfers between devices with their start and end apart: 3, of which 3 were waited for; matrix products, arithmetic and copies ran while one was open for 1% of the time, Pallas kernels for 0%

profile of v1, /device:TPU:1, one launch (start us, length us, event | category | flops | bytes accessed | tf_op | source)
XLA Modules:
  0.0 226.6 jit_solution(16403086268566574519)
XLA Ops:
  6.5 0.0 all-gather.3.cloned.1.call-start
  6.5 20.9 %all_gather.13 = bf16[128,3584]{1,0:T(8,128)(2,1)} all-gather(bf16[128,896]{1,0:T(8,128)(2,1)} %param.6), channel_id=1, replica_groups=mesh['node'=8,'group'=4] {'group'}, dimensions={1}, use_global_device_ids=true | all-gather | bytes 1146880 | tf_op jit(solution)/shard_map/all_gather | solution.py:70
  27.4 0.0 all-gather.3.cloned.1.call-update
  27.4 0.0 all-gather.5.cloned.1.call-start
  27.5 0.7 convert_multiply_fusion
  28.2 0.1 copy.10
  28.3 0.8 copy.9
  29.1 0.3 convolution_convert_fusion.1
  29.5 0.1 copy.11
  29.6 11.5 %all_gather.12 = bf16[1024,16]{0,1:T(8,128)(2,1)S(1)} all-gather(bf16[128,16]{0,1:T(8,128)(2,1)S(1)} %bitcast.10), channel_id=1, replica_groups=mesh['node'=8,'group'=4] {'node'}, dimensions={0}, use_global_device_ids=true | all-gather | bytes 36864 | tf_op jit(solution)/shard_map/all_gather | solution.py:69
  41.0 38.4 %all-gather.3.cloned.1.call-done = bf16[1024,3584]{1,0:T(8,128)(2,1)} async-done(((bf16[128,3584]{1,0:T(8,128)(2,1)}), bf16[1024,3584]{1,0:T(8,128)(2,1)}) %all-gather.3.cloned.1.call-update) | async-done | bytes 7340048 | tf_op jit(solution)/shard_map/all_gather | solution.py:71
  79.4 0.0 copy-start
  79.4 0.0 copy-start.1
  79.4 7.4 %fusion.1 = f32[1024,512]{1,0:T(8,128)S(1)} fusion(bf16[1024,3584]{1,0:T(8,128)(2,1)} %all-gather.3.cloned.1.call-done, bf16[3584,512]{1,0:T(8,128)(2,1)} %param.9), kind=kOutput, calls=%fused_computation.7 | convolution fusion | flops 3758096384 | bytes 13107200 | tf_op jit(solution)/shard_map/dot_general | solution.py:74
  86.9 0.0 copy-done
  86.9 0.0 copy-done.1
  86.9 5.2 %multiply_convert_fusion = bf16[1024,512]{1,0:T(8,128)(2,1)} fusion(f32[1024,512]{1,0:T(8,128)S(1)} %fusion.1, bf16[1024,3584]{1,0:T(8,128)(2,1)S(1)} %copy-done, bf16[3584,512]{1,0:T(8,128)(2,1)S(1)} %copy-done.1, f32[1024]{0:T(1024)S(1)} %bitcast.12), kind=kOutput, calls=%fused_computation | convolution fusion | flops 3761766400 | bytes 14159872 | tf_op jit(solution)/shard_map/dot_general | solution.py:75
  92.0 0.0 all-gather.5.cloned.1.call-update
  92.1 0.0 reduce-scatter.2.cloned.1.call-start
  92.1 80.5 %all-gather.5.cloned.1.call-done = bf16[1024,2048]{1,0:T(8,128)(2,1)} async-done(((bf16[1024,512]{1,0:T(8,128)(2,1)}), bf16[1024,2048]{1,0:T(8,128)(2,1)}) %all-gather.5.cloned.1.call-update) | async-done | bytes 4194320 | tf_op jit(solution)/shard_map/all_gather | solution.py:77
  172.6 9.1 %convolution_convert_fusion = bf16[1024,896]{1,0:T(8,128)(2,1)} fusion(bf16[1024,2048]{1,0:T(8,128)(2,1)} %all-gather.5.cloned.1.call-done, bf16[896,2048]{1,0:T(8,128)(2,1)} %param.11), kind=kOutput, calls=%fused_computation.1 | convolution fusion | flops 3759013888 | bytes 9699328 | tf_op jit(solution)/shard_map/dot_general | solution.py:79
  181.7 0.0 reduce-scatter.2.cloned.1.call-update
  181.7 38.3 %reduce-scatter.2.cloned.1.call-done = bf16[128,896]{1,0:T(8,128)(2,1)} async-done(((bf16[1024,896]{1,0:T(8,128)(2,1)}), bf16[128,896]{1,0:T(8,128)(2,1)}) %reduce-scatter.2.cloned.1.call-update) | async-done | bytes 229392 | tf_op jit(solution)/shard_map/reduce_scatter | solution.py:80
  (1 shorter events, 0.0 us)
Async XLA Ops:
  6.5 72.9 %all-gather.3.cloned.1.call-start = ((), (), s32[]{:S(2)}) async-start(), calls=%async_computation.1 | async-start | bytes 8257536 | tf_op jit(solution)/shard_map/all_gather | solution.py:71
  27.4 145.1 %all-gather.5.cloned.1.call-start = ((), (), s32[]{:S(2)}) async-start(), calls=%async_computation.2 | async-start | bytes 5242880 | tf_op jit(solution)/shard_map/all_gather | solution.py:77
  79.4 7.4 %copy-start = (bf16[1024,3584]{1,0:T(8,128)(2,1)S(1)}, bf16[1024,3584]{1,0:T(8,128)(2,1)}, u32[]{:S(2)}) copy-start(bf16[1024,3584]{1,0:T(8,128)(2,1)} %all-gather.3.cloned.1.call-done) | copy-start | bytes 22020100
  79.4 7.4 %copy-start.1 = (bf16[3584,512]{1,0:T(8,128)(2,1)S(1)}, bf16[3584,512]{1,0:T(8,128)(2,1)}, u32[]{:S(2)}) copy-start(bf16[3584,512]{1,0:T(8,128)(2,1)} %param.10) | copy-start | bytes 11010052
  92.1 128.0 %reduce-scatter.2.cloned.1.call-start = ((), (), s32[]{:S(2)}) async-start(), calls=%async_computation.3 | async-start | bytes 2064384 | tf_op jit(solution)/shard_map/reduce_scatter | solution.py:80
Sparse Core Ops, SparseCore 0:
  27.5 51.8 all-gather.2
  92.2 80.3 all-gather.4
  181.8 38.1 reduce-scatter.1

commit v2 on v1

--- a/solution.py
+++ b/solution.py
@@ -1,6 +1,10 @@
+import functools
+
 import jax
 import jax.numpy as jnp
 from jax import lax
+from jax.experimental import pallas as pl
+from jax.experimental.pallas import tpu as pltpu
 from jax.sharding import PartitionSpec as P
 
 F = 1024
@@ -63,6 +67,218 @@
     return jnp.einsum("tjm,tjk->tmk", hits, pairs).reshape(combine.shape[0], -1)
 
 
+def fused_kernel(tok_in, scl_in, wg_hbm, wu_hbm, wd_hbm, out,
+                 tok, scl, hid, part, inbox, wg, wu, wd, send, recv, local):
+    groups = lax.axis_size("group")
+    z, n = lax.axis_index("group"), lax.axis_index("node")
+    core, x, y = n % 2, (n // 2) % 2, n // 4
+    rows, width = tok_in.shape
+    hid_dev = wg.shape[1]
+
+    def partner(m):
+        flip = lambda bit, on: 1 - bit if on else bit
+        return (flip(y, m // 4 % 2) * 2 + flip(x, m // 2 % 2)) * 2 + flip(core, m % 2)
+
+    own, chip_x, chip_y, chip_d = (partner(m) // 2 for m in (0, 2, 4, 6))
+    ids, pending = {}, []
+
+    def there(d):
+        return None if d == 0 else jnp.logical_and(z + d >= 0, z + d < groups)
+
+    def guarded(conds, body):
+        conds = [c for c in conds if c is not None]
+        if conds:
+            pl.when(functools.reduce(jnp.logical_and, conds))(body)
+        else:
+            body()
+
+    def describe(key, src, dst, node, group):
+        i = ids.setdefault(key, len(ids))
+        return pltpu.make_async_remote_copy(
+            src_ref=src, dst_ref=dst, send_sem=send.at[i], recv_sem=recv.at[i],
+            device_id=(node, group), device_id_type=pl.DeviceIdType.MESH)
+
+    def push(key, ref, node, group=z, conds=(), dst=None):
+        ref_to = ref if dst is None else dst
+        make = lambda: describe(key, ref(), ref_to(), node, group)
+        ids.setdefault(key, len(ids))
+        guarded(conds, lambda: make().start())
+        pending.append((conds, make))
+
+    def arrive(key, ref, conds=()):
+        ids.setdefault(key, len(ids))
+        guarded(conds, lambda: describe(key, ref(), ref(), partner(1), z).wait_recv())
+
+    loads = [pltpu.make_async_copy(a, b, local.at[i])
+             for i, (a, b) in enumerate(((wg_hbm, wg), (wu_hbm, wu), (wd_hbm, wd)))]
+    for load in loads:
+        load.start()
+
+    barrier = pltpu.get_barrier_semaphore()
+    for m in range(1, 8):
+        pl.semaphore_signal(barrier, inc=1, device_id=(partner(m), z), device_id_type=pl.DeviceIdType.MESH)
+    for d in (-1, 1):
+        guarded([there(d)], lambda d=d: pl.semaphore_signal(
+            barrier, inc=1, device_id=(n, z + d), device_id_type=pl.DeviceIdType.MESH))
+    tok[own, core, z] = tok_in[...]
+    scl[own, core] = scl_in[...]
+    pl.semaphore_wait(barrier, 7 + (z + 2) // 3 + (groups + 1 - z) // 3)
+
+    def shard(chip, d):
+        return lambda: tok.at[chip, core, z + d]
+
+    half = rows // 2
+
+    def half_shard(chip, d, which):
+        return lambda: tok.at[chip, core, z + d, pl.ds(which * half, half)]
+
+    def spread(d):
+        for step in (-1, 1):
+            if d * step <= 0:
+                push(("t", step, abs(d)), shard(own, d), n, z + step, [c for c in (there(d), there(step)) if c is not None])
+        conds = [there(d)] if d else []
+        push(("x", d), shard(own, d), partner(2), conds=conds)
+        push(("y", d), shard(own, d), partner(4), conds=conds)
+
+    def turn(d):
+        conds = [there(d)] if d else []
+        arrive(("x", d), shard(chip_x, d), conds)
+        push(("dy", d), half_shard(chip_x, d, 0), partner(4), conds=conds)
+        arrive(("y", d), shard(chip_y, d), conds)
+        push(("dx", d), half_shard(chip_y, d, 1), partner(2), conds=conds)
+
+    spread(0)
+    for m in range(1, 8):
+        push(("scl", m), lambda: scl.at[own, core], partner(m))
+    for r in range(1, groups):
+        for d in (-r, r):
+            arrive(("t", 1 if d < 0 else -1, r - 1), shard(own, d), [there(d)])
+            spread(d)
+        for d in ((0,) if r == 1 else (1 - r, r - 1)):
+            turn(d)
+
+    def column(chip, c):
+        return lambda: tok.at[chip, c]
+
+    def swap(k, chip):
+        push(("sib", k), column(chip, core), partner(1))
+
+    swap(0, own)
+
+    def node_of(chip, c):
+        return lambda: scl.at[chip, c]
+
+    for load in loads:
+        load.wait()
+    for m in range(1, 8):
+        arrive(("scl", m), node_of(partner(m) // 2, partner(m) % 2))
+    expert = EXP_NODE * n + z * hid_dev // F
+    lanes = scl.shape[-1]
+    pick = (lax.broadcasted_iota(jnp.int32, (lanes, hid_dev), 0) == expert).astype(jnp.bfloat16)
+
+    def make_hidden(k, chip):
+        arrive(("sib", k), column(chip, 1 - core))
+        scale = jnp.dot(scl[chip].reshape(2 * rows, lanes), pick, preferred_element_type=jnp.float32)
+        gate = up = None
+        for g in range(groups):
+            block = tok[chip, :, g].reshape(2 * rows, width)
+            depth = pl.ds(g * width, width)
+            a = jnp.dot(block, wg[depth], preferred_element_type=jnp.float32)
+            b = jnp.dot(block, wu[depth], preferred_element_type=jnp.float32)
+            gate, up = (a, b) if g == 0 else (gate + a, up + b)
+        hid[chip, z] = (scale * (gate / (1.0 + jnp.exp(-gate))) * up).astype(jnp.bfloat16)
+        hop(k, chip, 0)
+
+    def hop(k, chip, d):
+        for step in (-1, 1):
+            if d * step <= 0:
+                push(("h", k, step, abs(d)), lambda: hid.at[chip, z + d], n, z + step,
+                     [c for c in (there(d), there(step)) if c is not None])
+
+    def relay(k, chip, r):
+        for d in (-r, r):
+            arrive(("h", k, 1 if d < 0 else -1, r - 1), lambda: hid.at[chip, z + d], [there(d)])
+            hop(k, chip, d)
+
+    def make_part(chip, ms):
+        total = None
+        for g in range(groups):
+            term = lax.dot_general(hid[chip, g], wd[:, pl.ds(g * hid_dev, hid_dev)], (((1,), (1,)), ((), ())),
+                                   preferred_element_type=jnp.float32)
+            total = term if g == 0 else total + term
+        part[chip] = total.astype(jnp.bfloat16).reshape(2, rows, width)
+        for m in ms:
+            push(("o", m), lambda m=m: part.at[chip, partner(m) % 2], partner(m), dst=lambda m=m: inbox.at[m])
+
+    make_hidden(0, own)
+    for d in (1 - groups, groups - 1):
+        turn(d)
+    swap(1, chip_x)
+    swap(2, chip_y)
+    relay(0, own, 1)
+    make_hidden(1, chip_x)
+    relay(0, own, 2)
+    make_hidden(2, chip_y)
+    relay(0, own, 3)
+    relay(1, chip_x, 1)
+    for d in [0] + [s * r for r in range(1, groups) for s in (-1, 1)]:
+        conds = [there(d)] if d else []
+        arrive(("dy", d), half_shard(chip_d, d, 0), conds)
+        arrive(("dx", d), half_shard(chip_d, d, 1), conds)
+    swap(3, chip_d)
+    relay(1, chip_x, 2)
+    relay(2, chip_y, 1)
+    make_hidden(3, chip_d)
+    relay(1, chip_x, 3)
+    make_part(own, (1,))
+    relay(2, chip_y, 2)
+    relay(3, chip_d, 1)
+    relay(2, chip_y, 3)
+    make_part(chip_x, (2, 3))
+    relay(3, chip_d, 2)
+    make_part(chip_y, (4, 5))
+    relay(3, chip_d, 3)
+    make_part(chip_d, (6, 7))
+    total = part[own, core].astype(jnp.float32)
+    for m in range(1, 8):
+        arrive(("o", m), lambda: inbox.at[m])
+        total = total + inbox[m].astype(jnp.float32)
+    out[...] = total.astype(jnp.bfloat16)
+    for conds, make in pending:
+        guarded(conds, lambda: make().wait_send())
+
+
+def fused_shards(tokens, node_routes, combine, w_gate, w_up, w_down):
+    rows, width = tokens.shape
+    groups, nodes = lax.axis_size("group"), lax.axis_size("node")
+    hid_dev = w_gate.shape[1]
+    scales = pair_scales(node_routes, combine)
+    scales = jnp.pad(scales, ((0, 0), (0, 128 - scales.shape[1]))).astype(jnp.bfloat16)
+    vmem, hbm = pl.BlockSpec(memory_space=pltpu.VMEM), pl.BlockSpec(memory_space=pl.ANY)
+    low = jnp.bfloat16
+    return pl.pallas_call(
+        fused_kernel,
+        out_shape=jax.ShapeDtypeStruct((rows, width), low),
+        in_specs=[vmem, vmem, hbm, hbm, hbm],
+        out_specs=vmem,
+        scratch_shapes=[
+            pltpu.VMEM((nodes // 2, 2, groups, rows, width), low),
+            pltpu.VMEM((nodes // 2, 2, rows, 128), low),
+            pltpu.VMEM((nodes // 2, groups, 2 * rows, hid_dev), low),
+            pltpu.VMEM((nodes // 2, 2, rows, width), low),
+            pltpu.VMEM((nodes, rows, width), low),
+            pltpu.VMEM(w_gate.shape, low),
+            pltpu.VMEM(w_up.shape, low),
+            pltpu.VMEM(w_down.shape, low),
+            pltpu.SemaphoreType.DMA((96,)),
+            pltpu.SemaphoreType.DMA((96,)),
+            pltpu.SemaphoreType.DMA((3,)),
+        ],
+        compiler_params=pltpu.CompilerParams(
+            collective_id=0, has_side_effects=True, vmem_limit_bytes=56 * 1024 * 1024),
+    )(tokens, scales, w_gate, w_up, w_down)
+
+
 def dense_shards(tokens, node_routes, combine, w_gate, w_up, w_down):
     hid_dev = w_gate.shape[1]
     scales = pair_scales(node_routes, combine).astype(jnp.bfloat16)
@@ -82,6 +298,8 @@
 
 def shards(tokens, node_routes, *rest):
     slots = 2 * tokens.shape[0] * node_routes.shape[1] // lax.axis_size("node")
+    if slots == tokens.shape[0] and lax.axis_size("node") == 8 and lax.axis_size("group") == 4:
+        return fused_shards(tokens, node_routes, *rest)
     if slots == tokens.shape[0]:
         return dense_shards(tokens, node_routes, *rest)
     return routed_shards(tokens, node_routes, *rest)

time: 227 us -> 133 us (0.59)
  waiting for transfers between devices: 157 us -> 0 us
  Pallas kernels: 0 us -> 128 us
  blocking collectives: 32.3 us -> 0 us
  matrix products: 22 us -> 0.35 us
  between operations: 13.2 us -> 0.02 us
  local copies, waits for them, and re-layouts: 1.01 us -> 3.42 us
    pallas_call x0 -> x1, Pallas kernels: none -> 128 us  [fused_shards(): pl.pallas_call(fused_kernel, out_shape=jax.ShapeDtypeStruct((rows, width)...]
    all_gather x2 -> x0, waiting for transfers between devices: 119 us -> none  [the longest x1 80.5 us: dense_shards(): all_hidden = lax.all_gather(hidden, 'group', axis=1, tiled=True)]
    reduce_scatter x1 -> x0, waiting for transfers between devices: 38.3 us -> none  [dense_shards(): lax.psum_scatter(part.astype(jnp.bfloat16), 'node', scatter_dimension=0,...]
    all_gather x2 -> x0, blocking collectives: 32.3 us -> none  [the longest x1 20.9 us: dense_shards(): column = lax.all_gather(tokens, 'group', axis=1, tiled=True)]
    dot_general x3 -> x0, matrix products: 21.7 us -> none  [the longest x1 9.1 us: dense_shards(): lax.dot_general(all_hidden, w_down, contract, preferred_element_type=jnp....]
  transfers between devices with their start and end apart: 3 -> 0, of which waited for: 3 -> 0; matrix products, arithmetic and copies ran while one was open for 1% -> 0% of each run, Pallas kernels for 0% -> 0%
where the time goes in v2:
time: 133 us; the launch traced here: 132 us
  Pallas kernels  128 us (96%)
  local copies, waits for them, and re-layouts  3.42 us (3%)
    pallas_call x1, Pallas kernels, fused_shards(): pl.pallas_call(fused_kernel, out_shape=jax.ShapeDtypeStruct((rows, width)...  128 us

profile of v2, /device:TPU:1, one launch (start us, length us, event | category | flops | bytes accessed | tf_op | source)
XLA Modules:
  0.0 132.3 jit_solution(5828378359305068799)
XLA Ops:
  0.0 0.7 convert_multiply_fusion
  0.7 0.1 copy.11
  0.8 0.8 copy.10
  1.6 0.3 convolution_convert_fusion
  2.0 0.1 copy.12
  2.1 0.1 copy.13
  2.2 0.6 pad.5.scl_in
  2.8 127.8 %shard_map.64 = bf16[128,896]{1,0:T(8,128)(2,1)} custom-call(bf16[128,896]{1,0:T(8,128)(2,1)} %tok_in.1, bf16[128,128]{1,0:T(8,128)(2,1)} %pad.5.scl_in, bf16[3584,512]{1,0:T(8,128)(2,1)} %wg_hbm.1, bf16[3584,512]{1,0:T(8,128)(2,1)} %wu_hbm.1, bf16[896,2048]{1,0:T(8,128)(2,1)} %wd_hbm.1), custom_call_target="tpu_custom_call" | custom-call | tf_op jit(solution)/shard_map/pallas_call | solution.py:259
  130.7 1.6 %copy.15 = bf16[128,896]{1,0:T(8,128)(2,1)} copy(bf16[128,896]{1,0:T(8,128)(2,1)} %shard_map.64) | data formatting | bytes 458752

commit v3 on v2

--- a/solution.py
+++ b/solution.py
@@ -176,69 +176,91 @@
     lanes = scl.shape[-1]
     pick = (lax.broadcasted_iota(jnp.int32, (lanes, hid_dev), 0) == expert).astype(jnp.bfloat16)
 
-    def make_hidden(k, chip):
-        arrive(("sib", k), column(chip, 1 - core))
-        scale = jnp.dot(scl[chip].reshape(2 * rows, lanes), pick, preferred_element_type=jnp.float32)
+    def make_hidden(k, chip, first, count):
+        if k < 4:
+            arrive(("sib", k), column(chip, 1 - core))
+        cores = pl.ds(first, count)
+        scale = jnp.dot(scl[chip, cores].reshape(count * rows, lanes), pick, preferred_element_type=jnp.float32)
         gate = up = None
         for g in range(groups):
-            block = tok[chip, :, g].reshape(2 * rows, width)
+            block = tok[chip, cores, g].reshape(count * rows, width)
             depth = pl.ds(g * width, width)
             a = jnp.dot(block, wg[depth], preferred_element_type=jnp.float32)
             b = jnp.dot(block, wu[depth], preferred_element_type=jnp.float32)
             gate, up = (a, b) if g == 0 else (gate + a, up + b)
-        hid[chip, z] = (scale * (gate / (1.0 + jnp.exp(-gate))) * up).astype(jnp.bfloat16)
-        hop(k, chip, 0)
-
-    def hop(k, chip, d):
+        chunk = pl.ds(first * rows, count * rows)
+        hid[chip, z, chunk] = (scale * (gate / (1.0 + jnp.exp(-gate))) * up).astype(jnp.bfloat16)
+        hop((k, chip, first, count), 0)
+
+    def hop(piece, d):
+        k, chip, first, count = piece
         for step in (-1, 1):
             if d * step <= 0:
-                push(("h", k, step, abs(d)), lambda: hid.at[chip, z + d], n, z + step,
+                push(("h", k, step, abs(d)),
+                     lambda: hid.at[chip, z + d, pl.ds(first * rows, count * rows)], n, z + step,
                      [c for c in (there(d), there(step)) if c is not None])
 
-    def relay(k, chip, r):
+    def relay(piece, r):
+        k, chip, first, count = piece
         for d in (-r, r):
-            arrive(("h", k, 1 if d < 0 else -1, r - 1), lambda: hid.at[chip, z + d], [there(d)])
-            hop(k, chip, d)
-
-    def make_part(chip, ms):
+            arrive(("h", k, 1 if d < 0 else -1, r - 1),
+                   lambda: hid.at[chip, z + d, pl.ds(first * rows, count * rows)], [there(d)])
+            hop(piece, d)
+
+    def make_part(piece, ms):
+        k, chip, first, count = piece
         total = None
         for g in range(groups):
-            term = lax.dot_general(hid[chip, g], wd[:, pl.ds(g * hid_dev, hid_dev)], (((1,), (1,)), ((), ())),
+            term = lax.dot_general(hid[chip, g, pl.ds(first * rows, count * rows)],
+                                   wd[:, pl.ds(g * hid_dev, hid_dev)], (((1,), (1,)), ((), ())),
                                    preferred_element_type=jnp.float32)
             total = term if g == 0 else total + term
-        part[chip] = total.astype(jnp.bfloat16).reshape(2, rows, width)
+        part[chip, pl.ds(first, count)] = total.astype(jnp.bfloat16).reshape(count, rows, width)
         for m in ms:
-            push(("o", m), lambda m=m: part.at[chip, partner(m) % 2], partner(m), dst=lambda m=m: inbox.at[m])
-
-    make_hidden(0, own)
+            conds = [core != first] if m == 1 else []
+            push(("o", m), lambda m=m: part.at[chip, partner(m) % 2], partner(m), conds=conds,
+                 dst=lambda m=m: inbox.at[m])
+
+    own_a, col_x, col_y, col_d, own_b = (
+        (0, own, 0, 1), (1, chip_x, 0, 2), (2, chip_y, 0, 2), (3, chip_d, 0, 2), (4, own, 1, 1))
+
+    def diagonal():
+        for d in [0] + [s * r for r in range(1, groups) for s in (-1, 1)]:
+            conds = [there(d)] if d else []
+            arrive(("dy", d), half_shard(chip_d, d, 0), conds)
+            arrive(("dx", d), half_shard(chip_d, d, 1), conds)
+        swap(3, chip_d)
+
+    make_hidden(*own_a)
     for d in (1 - groups, groups - 1):
         turn(d)
     swap(1, chip_x)
     swap(2, chip_y)
-    relay(0, own, 1)
-    make_hidden(1, chip_x)
-    relay(0, own, 2)
-    make_hidden(2, chip_y)
-    relay(0, own, 3)
-    relay(1, chip_x, 1)
-    for d in [0] + [s * r for r in range(1, groups) for s in (-1, 1)]:
-        conds = [there(d)] if d else []
-        arrive(("dy", d), half_shard(chip_d, d, 0), conds)
-        arrive(("dx", d), half_shard(chip_d, d, 1), conds)
-    swap(3, chip_d)
-    relay(1, chip_x, 2)
-    relay(2, chip_y, 1)
-    make_hidden(3, chip_d)
-    relay(1, chip_x, 3)
-    make_part(own, (1,))
-    relay(2, chip_y, 2)
-    relay(3, chip_d, 1)
-    relay(2, chip_y, 3)
-    make_part(chip_x, (2, 3))
-    relay(3, chip_d, 2)
-    make_part(chip_y, (4, 5))
-    relay(3, chip_d, 3)
-    make_part(chip_d, (6, 7))
+    make_hidden(*col_x)
+    make_hidden(*col_y)
+    relay(own_a, 1)
+    relay(own_a, 2)
+    relay(own_a, 3)
+    relay(col_x, 1)
+    relay(col_x, 2)
+    relay(col_x, 3)
+    diagonal()
+    make_hidden(*col_d)
+    relay(col_y, 1)
+    make_hidden(*own_b)
+    relay(col_y, 2)
+    relay(col_y, 3)
+    make_part(own_a, (1,))
+    make_part(col_x, (2, 3))
+    relay(col_d, 1)
+    relay(col_d, 2)
+    make_part(col_y, (4, 5))
+    relay(col_d, 3)
+    relay(own_b, 1)
+    relay(own_b, 2)
+    make_part(col_d, (6, 7))
+    relay(own_b, 3)
+    make_part(own_b, (1,))
     total = part[own, core].astype(jnp.float32)
     for m in range(1, 8):
         arrive(("o", m), lambda: inbox.at[m])

time: 133 us -> 125 us (0.940)
  Pallas kernels: 128 us -> 121 us
    pallas_call x1, Pallas kernels: 128 us -> 121 us  [fused_shards(): pl.pallas_call(fused_kernel, out_shape=jax.ShapeDtypeStruct((rows, width)...]
where the time goes in v3:
time: 125 us
  Pallas kernels  121 us (97%)
  local copies, waits for them, and re-layouts  3.42 us (3%)
    pallas_call x1, Pallas kernels, fused_shards(): pl.pallas_call(fused_kernel, out_shape=jax.ShapeDtypeStruct((rows, width)...  121 us

profile of v3, /device:TPU:1, one launch (start us, length us, event | category | flops | bytes accessed | tf_op | source)
XLA Modules:
  0.0 125.2 jit_solution(12997541348715338162)
XLA Ops:
  0.0 0.7 convert_multiply_fusion
  0.7 0.1 copy.11
  0.8 0.8 copy.10
  1.6 0.3 convolution_convert_fusion
  2.0 0.1 copy.12
  2.1 0.1 copy.13
  2.2 0.6 pad.5.scl_in
  2.8 120.8 %shard_map.64 = bf16[128,896]{1,0:T(8,128)(2,1)} custom-call(bf16[128,896]{1,0:T(8,128)(2,1)} %tok_in.1, bf16[128,128]{1,0:T(8,128)(2,1)} %pad.5.scl_in, bf16[3584,512]{1,0:T(8,128)(2,1)} %wg_hbm.1, bf16[3584,512]{1,0:T(8,128)(2,1)} %wu_hbm.1, bf16[896,2048]{1,0:T(8,128)(2,1)} %wd_hbm.1), custom_call_target="tpu_custom_call" | custom-call | tf_op jit(solution)/shard_map/pallas_call | solution.py:281
  123.6 1.6 %copy.15 = bf16[128,896]{1,0:T(8,128)(2,1)} copy(bf16[128,896]{1,0:T(8,128)(2,1)} %shard_map.64) | data formatting | bytes 458752

commit v4 on v3

--- a/solution.py
+++ b/solution.py
@@ -217,12 +217,14 @@
             total = term if g == 0 else total + term
         part[chip, pl.ds(first, count)] = total.astype(jnp.bfloat16).reshape(count, rows, width)
         for m in ms:
-            conds = [core != first] if m == 1 else []
+            conds = []
+            if count == 1:
+                conds = [core == first if m % 2 == 0 else core != first]
             push(("o", m), lambda m=m: part.at[chip, partner(m) % 2], partner(m), conds=conds,
                  dst=lambda m=m: inbox.at[m])
 
-    own_a, col_x, col_y, col_d, own_b = (
-        (0, own, 0, 1), (1, chip_x, 0, 2), (2, chip_y, 0, 2), (3, chip_d, 0, 2), (4, own, 1, 1))
+    own_a, col_x, col_y, dia_a, own_b, dia_b = (
+        (0, own, 0, 1), (1, chip_x, 0, 2), (2, chip_y, 0, 2), (3, chip_d, 0, 1), (4, own, 1, 1), (5, chip_d, 1, 1))
 
     def diagonal():
         for d in [0] + [s * r for r in range(1, groups) for s in (-1, 1)]:
@@ -232,35 +234,40 @@
         swap(3, chip_d)
 
     make_hidden(*own_a)
+    make_hidden(*own_b)
     for d in (1 - groups, groups - 1):
         turn(d)
     swap(1, chip_x)
     swap(2, chip_y)
+    relay(own_a, 1)
     make_hidden(*col_x)
     make_hidden(*col_y)
-    relay(own_a, 1)
     relay(own_a, 2)
     relay(own_a, 3)
+    relay(own_b, 1)
+    relay(own_b, 2)
+    relay(own_b, 3)
+    diagonal()
+    make_hidden(*dia_a)
+    make_hidden(*dia_b)
     relay(col_x, 1)
     relay(col_x, 2)
     relay(col_x, 3)
-    diagonal()
-    make_hidden(*col_d)
+    make_part(own_a, (1,))
+    make_part(own_b, (1,))
     relay(col_y, 1)
-    make_hidden(*own_b)
+    make_part(col_x, (2, 3))
     relay(col_y, 2)
     relay(col_y, 3)
-    make_part(own_a, (1,))
-    make_part(col_x, (2, 3))
-    relay(col_d, 1)
-    relay(col_d, 2)
+    relay(dia_a, 1)
+    relay(dia_a, 2)
     make_part(col_y, (4, 5))
-    relay(col_d, 3)
-    relay(own_b, 1)
-    relay(own_b, 2)
-    make_part(col_d, (6, 7))
-    relay(own_b, 3)
-    make_part(own_b, (1,))
+    relay(dia_a, 3)
+    relay(dia_b, 1)
+    relay(dia_b, 2)
+    make_part(dia_a, (6, 7))
+    relay(dia_b, 3)
+    make_part(dia_b, (6, 7))
     total = part[own, core].astype(jnp.float32)
     for m in range(1, 8):
         arrive(("o", m), lambda: inbox.at[m])
@@ -292,8 +299,8 @@
             pltpu.VMEM(w_gate.shape, low),
             pltpu.VMEM(w_up.shape, low),
             pltpu.VMEM(w_down.shape, low),
-            pltpu.SemaphoreType.DMA((96,)),
-            pltpu.SemaphoreType.DMA((96,)),
+            pltpu.SemaphoreType.DMA((128,)),
+            pltpu.SemaphoreType.DMA((128,)),
             pltpu.SemaphoreType.DMA((3,)),
         ],
         compiler_params=pltpu.CompilerParams(

time: 125 us -> 128 us (1.024)
  Pallas kernels: 121 us -> 123 us
    pallas_call x1, Pallas kernels: 121 us -> 123 us  [fused_shards(): pl.pallas_call(fused_kernel, out_shape=jax.ShapeDtypeStruct((rows, width)...]
where the time goes in v4:
time: 128 us
  Pallas kernels  123 us (96%)
  local copies, waits for them, and re-layouts  3.42 us (3%)
    pallas_call x1, Pallas kernels, fused_shards(): pl.pallas_call(fused_kernel, out_shape=jax.ShapeDtypeStruct((rows, width)...  123 us

profile of v4, /device:TPU:1, one launch (start us, length us, event | category | flops | bytes accessed | tf_op | source)
XLA Modules:
  0.0 127.5 jit_solution(7718977104267588122)
XLA Ops:
  0.0 0.7 convert_multiply_fusion
  0.7 0.1 copy.11
  0.8 0.8 copy.10
  1.6 0.3 convolution_convert_fusion
  2.0 0.1 copy.12
  2.1 0.1 copy.13
  2.2 0.6 pad.5.scl_in
  2.8 123.1 %shard_map.64 = bf16[128,896]{1,0:T(8,128)(2,1)} custom-call(bf16[128,896]{1,0:T(8,128)(2,1)} %tok_in.1, bf16[128,128]{1,0:T(8,128)(2,1)} %pad.5.scl_in, bf16[3584,512]{1,0:T(8,128)(2,1)} %wg_hbm.1, bf16[3584,512]{1,0:T(8,128)(2,1)} %wu_hbm.1, bf16[896,2048]{1,0:T(8,128)(2,1)} %wd_hbm.1), custom_call_target="tpu_custom_call" | custom-call | tf_op jit(solution)/shard_map/pallas_call | solution.py:288
  125.9 1.6 %copy.15 = bf16[128,896]{1,0:T(8,128)(2,1)} copy(bf16[128,896]{1,0:T(8,128)(2,1)} %shard_map.64) | data formatting | bytes 458752
